TPU v7x, 32 devices: a whole 2x2x4 slice. The times are simulated.
32 devices in a mesh: groups: 2 (over x), wide: 8 (over z, y), narrow: 2 (over core).
Axes of the slice: x: 2, y: 2, z: 4, core: 2. Of those that a mesh axis runs over, the one named last changes fastest.
Arguments:
- tokens: bfloat16 [2048, 2048], P(('groups', 'wide', 'narrow')), parts along dimension 0, may hold values from -6 to 6
- gate_wts: bfloat16 [2048, 8], P(('groups', 'wide', 'narrow')), parts along dimension 0, may hold values from 0.099609375 to 1
- expert_ids: int32 [2048, 8], P(('groups', 'wide', 'narrow')), parts along dimension 0, may hold values from 0 to 23, as said below
- replica: int32 [2048, 8], P(('groups', 'wide', 'narrow')), parts along dimension 0, may hold values from 0 to 1, as said below
- w_gate: bfloat16 [32, 2048, 384], P(('wide', 'narrow')), may hold values from -0.125 to 0.125
- w_up: bfloat16 [32, 2048, 384], P(('wide', 'narrow')), may hold values from -0.125 to 0.125
- w_down: bfloat16 [32, 384, 2048], P(('wide', 'narrow')), may hold values from -0.3125 to 0.3125
- queries: bfloat16 [64, 32, 128], P(('groups', 'wide', 'narrow')), parts along dimension 0, may hold values from -80 to 80
- k_cache: bfloat16 [64, 640, 4, 128], P(('groups', 'wide', 'narrow')), parts along dimension 0, may hold values from -4 to 4
- value_cache: bfloat16 [64, 640, 4, 128], P(('groups', 'wide', 'narrow')), parts along dimension 0, may hold values from -5 to 5
- lengths: int32 [64], P(('groups', 'wide', 'narrow')), parts along dimension 0, may hold values from 80 to 640, as said below
Outputs:
- routed_out: bfloat16 [2048, 2048], P(('groups', 'wide', 'narrow')), parts along dimension 0
- attn_out: bfloat16 [64, 4096], P(('groups', 'wide', 'narrow')), parts along dimension 0
There are 2 independent parts, one for each index of `groups`. A program takes and returns all parts, laid end to end along the dimension named above; an argument that names none is the same for every part. Nothing has to cross between parts.
Inputs may be any that keep to these rules, and one draw needn't show every extreme that they name: `expert_ids`: each row names 8 different experts. Counted over the rows of one device (aligned blocks of 64 rows), the rows whose slots lie on one device number at most 64; one device, the same for every block of a draw, gets exactly 64 rows from every block. `replica`: 1 only where the named expert is below 8. `lengths`: one request of each draw has exactly 640 live positions.
All inputs are finite; a program needn't handle non-finite values.
Results may differ from a plain program's by a relative error of at most 0.008.
Values may be sent and summed in bfloat16 or wider, within the bound.
A program may use at most 128 MiB of HBM per device.

v0:
```python
import jax
import jax.numpy as jnp
from jax import lax
from jax.sharding import PartitionSpec as P

SLOT_DEV = 2


def attend(queries, k_cache, value_cache, lengths):
    reqs, heads, head_dim = queries.shape
    kv_heads = k_cache.shape[2]
    group = heads // kv_heads
    grouped = queries.reshape(reqs, kv_heads, group, head_dim)
    scores = jnp.einsum(
        "rkgd,rlkd->rkgl", grouped, k_cache, preferred_element_type=jnp.float32
    ) * head_dim ** (-0.5)
    valid = jnp.arange(k_cache.shape[1], dtype=jnp.int32)[None, :] < lengths[:, None]
    valid = valid[:, None, None, :]
    scores = jnp.where(valid, scores, -1e30)
    top = jnp.max(scores, axis=-1, keepdims=True)
    expd = jnp.where(valid, jnp.exp(scores - top), 0.0)
    probs = (expd / jnp.sum(expd, axis=-1, keepdims=True)).astype(jnp.bfloat16)
    mixed = jnp.einsum("rkgl,rlkd->rkgd", probs, value_cache, preferred_element_type=jnp.float32)
    return mixed.astype(jnp.bfloat16).reshape(reqs, heads * head_dim)


def local(
    tokens,
    gate_wts,
    expert_ids,
    replica,
    w_gate,
    w_up,
    w_down,
    queries,
    k_cache,
    value_cache,
    lengths,
):
    wide_count = lax.axis_size("wide")
    narrow_count = lax.axis_size("narrow")
    devices = wide_count * narrow_count
    experts = 3 * devices // 2
    spares = devices // 2
    rows_here = tokens.shape[0]
    model_width = tokens.shape[1]
    top_count = expert_ids.shape[1]
    capacity = min(rows_here, 2 * rows_here * top_count // devices)
    phys_slot = jnp.where((replica == 1) & (expert_ids < spares), expert_ids + experts, expert_ids)
    owner_dev = phys_slot // SLOT_DEV
    slot_bit = phys_slot % SLOT_DEV
    owners = jnp.arange(devices, dtype=jnp.int32)
    hits_mask = owner_dev[:, :, None] == owners[None, None, :]
    routed_to = jnp.any(hits_mask, axis=1).astype(jnp.float32)
    gate_values = gate_wts.astype(jnp.float32)
    coefficients = jnp.stack(
        [
            jnp.sum(
                jnp.where(hits_mask & (slot_bit[:, :, None] == j), gate_values[:, :, None], 0.0),
                axis=1,
            )
            for j in range(SLOT_DEV)
        ],
        axis=-1,
    )
    row_ids = jnp.arange(rows_here, dtype=jnp.int32)
    earlier = (row_ids[None, :] < row_ids[:, None]).astype(jnp.float32)
    before = jnp.dot(earlier, routed_to, precision=lax.Precision.HIGHEST)
    positions = jnp.arange(capacity, dtype=jnp.float32)
    slots_map = (routed_to[:, :, None] * (before[:, :, None] == positions[None, None, :])).astype(
        jnp.bfloat16
    )
    outgoing = jnp.einsum(
        "rdc,rm->dcm", slots_map, tokens, preferred_element_type=jnp.float32
    ).astype(jnp.bfloat16)
    weights_out = jnp.einsum(
        "rdc,rdj->dcj",
        slots_map,
        coefficients.astype(jnp.bfloat16),
        preferred_element_type=jnp.float32,
    ).astype(jnp.bfloat16)
    arrived = lax.all_to_all(outgoing, ("wide", "narrow"), split_axis=0, concat_axis=0, tiled=True)
    shares = lax.all_to_all(
        weights_out, ("wide", "narrow"), split_axis=0, concat_axis=0, tiled=True
    )
    flat = arrived.reshape(-1, model_width)
    share_flat = shares.reshape(-1, SLOT_DEV).astype(jnp.float32)
    result = jnp.zeros(flat.shape, jnp.float32)
    for j in range(SLOT_DEV):
        gated = jnp.dot(flat, w_gate[j], preferred_element_type=jnp.float32)
        upward = jnp.dot(flat, w_up[j], preferred_element_type=jnp.float32)
        hidden = (jax.nn.silu(gated) * upward).astype(jnp.bfloat16)
        result = result + share_flat[:, j : j + 1] * jnp.dot(
            hidden, w_down[j], preferred_element_type=jnp.float32
        )
    returned = lax.all_to_all(
        result.astype(jnp.bfloat16).reshape(arrived.shape),
        ("wide", "narrow"),
        split_axis=0,
        concat_axis=0,
        tiled=True,
    )
    attn_out = attend(queries, k_cache, value_cache, lengths)
    routed_out = jnp.einsum(
        "rdc,dcm->rm", slots_map, returned, preferred_element_type=jnp.float32
    ).astype(jnp.bfloat16)
    return (routed_out, attn_out)


def solution(mesh):
    in_specs = (
        P(("groups", "wide", "narrow"), None),
        P(("groups", "wide", "narrow"), None),
        P(("groups", "wide", "narrow"), None),
        P(("groups", "wide", "narrow"), None),
        P(("wide", "narrow"), None, None),
        P(("wide", "narrow"), None, None),
        P(("wide", "narrow"), None, None),
        P(("groups", "wide", "narrow"), None, None),
        P(("groups", "wide", "narrow"), None, None, None),
        P(("groups", "wide", "narrow"), None, None, None),
        P(("groups", "wide", "narrow")),
    )
    out_specs = (P(("groups", "wide", "narrow"), None), P(("groups", "wide", "narrow"), None))
    return jax.shard_map(local, mesh=mesh, in_specs=in_specs, out_specs=out_specs, check_vma=False)
```

profile of v0, /device:TPU:13, one launch (start us, length us, event | category | flops | bytes accessed | tf_op | source)
XLA Modules:
  0.0 247.4 jit_solution(1507079375398638786)
XLA Ops:
  0.6 0.0 copy-start
  0.6 0.8 add_select_fusion.1
  1.5 0.1 fusion.61
  1.6 0.7 broadcast_compare_fusion.1
  2.4 0.7 convert_element_type.48
  3.1 1.1 convolution_convert_fusion.1
  4.2 6.6 %all-to-all-start = ((bf16[16,64,2]{1,2,0:T(2,128)(2,1)}), bf16[16,64,2]{1,2,0:T(2,128)(2,1)S(1)}, u32[]{:S(2)}, u32[]{:S(2)}) async-start(bf16[16,64,2]{1,2,0:T(2,128)(2,1)} %convolution_convert_fusion.1), calls=%async_computation | async-start | bytes 16384 | tf_op jit(solution)/shard_map/all_to_all | solution.py:83
  10.7 4.6 %convolution_convert_fusion = bf16[16,64,2048]{2,1,0:T(8,128)(2,1)} fusion(bf16[64,2048]{1,0:T(8,128)(2,1)} %param.11, bf16[64,16]{0,1:T(8,128)(2,1)S(1)} %convert_element_type.46, f32[64,16]{0,1:T(8,128)S(1)} %fusion.61), kind=kOutput, calls=%fused_computation.2 | convolution fusion | flops 270663680 | bytes 4462592 | tf_op jit(solution)/shard_map/rdc,rm->dcm/dot_general | solution.py:73
  15.4 0.0 all-to-all-done
  15.4 6.1 %all-to-all-start.1 = ((bf16[16,64,2048]{2,1,0:T(8,128)(2,1)}), bf16[16,64,2048]{2,1,0:T(8,128)(2,1)}, u32[]{:S(2)}, u32[]{:S(2)}) async-start(bf16[16,64,2048]{2,1,0:T(8,128)(2,1)} %convolution_convert_fusion), calls=%async_computation.1 | async-start | bytes 8388608 | tf_op jit(solution)/shard_map/all_to_all | solution.py:82
  21.5 0.1 reshape.52
  21.6 92.4 %all-to-all-done.1 = bf16[16,64,2048]{2,1,0:T(8,128)(2,1)} async-done(((bf16[16,64,2048]{2,1,0:T(8,128)(2,1)}), bf16[16,64,2048]{2,1,0:T(8,128)(2,1)}, u32[]{:S(2)}, u32[]{:S(2)}) %all-to-all-start.1) | async-done | bytes 4194336 | tf_op jit(solution)/shard_map/all_to_all | solution.py:82
  114.0 6.3 %fusion.11 = f32[1024,384]{1,0:T(8,128)} fusion(bf16[1024,2048]{1,0:T(8,128)(2,1)} %bitcast.4, bf16[2,2048,384]{2,1,0:T(8,128)(2,1)} %param.15), kind=kOutput, calls=%fused_computation.14 | convolution fusion | flops 1610612736 | bytes 7340032 | tf_op jit(solution)/shard_map/dot_general | solution.py:90
  120.3 4.5 %fusion.5 = f32[1024,384]{1,0:T(8,128)S(1)} fusion(bf16[1024,2048]{1,0:T(8,128)(2,1)} %bitcast.4, bf16[2,2048,384]{2,1,0:T(8,128)(2,1)S(1)} %copy-done.2), kind=kOutput, calls=%fused_computation.8 | convolution fusion | flops 1610612736 | bytes 7340032 | tf_op jit(solution)/shard_map/dot_general | solution.py:90
  124.8 11.3 %fusion.7 = f32[1024,2048]{1,0:T(8,128)} fusion(bf16[2,384,2048]{2,1,0:T(8,128)(2,1)} %param.17, f32[1024,384]{1,0:T(8,128)} %fusion.11, bf16[1024,2048]{1,0:T(8,128)(2,1)} %bitcast.4, bf16[2,2048,384]{2,1,0:T(8,128)(2,1)} %param.16), kind=kOutput, calls=%fused_computation.10 | convolution fusion | flops 3223584768 | bytes 17301504 | tf_op jit(solution)/shard_map/dot_general | solution.py:93
  136.1 9.8 %add_convert_fusion = bf16[1024,2048]{1,0:T(8,128)(2,1)} fusion(f32[1024,2048]{1,0:T(8,128)} %fusion.7, f32[1024]{0:T(1024)S(1)} %bitcast.67, f32[1024]{0:T(1024)S(1)} %bitcast.66, bf16[2,384,2048]{2,1,0:T(8,128)(2,1)} %param.17, f32[1024,384]{1,0:T(8,128)S(1)} %fusion.5, bf16[1024,2048]{1,0:T(8,128)(2,1)} %bitcast.4, bf16[2,2048,384]{2,1,0:T(8,128)(2,1)} %param.16), kind=kOutput, calls=%fused_computation.1 | convolution fusion | flops 3231973376 | bytes 21504000 | tf_op jit(solution)/shard_map/dot_general | solution.py:93
  146.0 5.0 %all-to-all-start.2 = ((bf16[16,64,2048]{2,1,0:T(8,128)(2,1)}), bf16[16,64,2048]{2,1,0:T(8,128)(2,1)}, u32[]{:S(2)}, u32[]{:S(2)}) async-start(bf16[16,64,2048]{2,1,0:T(8,128)(2,1)} %bitcast.62), calls=%async_computation.2 | async-start | bytes 8388608 | tf_op jit(solution)/shard_map/all_to_all | solution.py:96
  151.0 0.1 iota_compare_fusion.4
  151.1 0.0 copy-done.4
  151.1 0.7 fusion.75
  151.8 0.4 fusion.41
  152.1 0.6 copy.66
  152.8 90.7 %all-to-all-done.2 = bf16[16,64,2048]{2,1,0:T(8,128)(2,1)} async-done(((bf16[16,64,2048]{2,1,0:T(8,128)(2,1)}), bf16[16,64,2048]{2,1,0:T(8,128)(2,1)}, u32[]{:S(2)}, u32[]{:S(2)}) %all-to-all-start.2) | async-done | bytes 4194336 | tf_op jit(solution)/shard_map/all_to_all | solution.py:96
  243.5 3.9 %fusion.1 = bf16[64,2048]{1,0:T(8,128)(2,1)} fusion(bf16[16,64,2048]{2,1,0:T(8,128)(2,1)} %all-to-all-done.2, bf16[64,16]{0,1:T(8,128)(2,1)S(1)} %convert_element_type.46, f32[64,16]{0,1:T(8,128)S(1)} %fusion.61), kind=kOutput, calls=%fused_computation.4 | convolution fusion | flops 268697600 | bytes 4462592 | tf_op jit(solution)/shard_map/rdc,dcm->rm/dot_general | solution.py:104
  (16 shorter events, 0.1 us)
Async XLA Ops:
  0.6 150.4 %copy-start = (bf16[2,640,4,128]{3,2,1,0:T(4,128)(2,1)S(1)}, bf16[2,640,4,128]{3,2,1,0:T(4,128)(2,1)}, u32[]{:S(2)}) copy-start(bf16[2,640,4,128]{3,2,1,0:T(4,128)(2,1)} %param.19) | copy-start | bytes 3932164
  4.2 11.2 %all-to-all-start = ((bf16[16,64,2]{1,2,0:T(2,128)(2,1)}), bf16[16,64,2]{1,2,0:T(2,128)(2,1)S(1)}, u32[]{:S(2)}, u32[]{:S(2)}) async-start(bf16[16,64,2]{1,2,0:T(2,128)(2,1)} %convolution_convert_fusion.1), calls=%async_computation | async-start | bytes 16384 | tf_op jit(solution)/shard_map/all_to_all | solution.py:83
  15.4 98.6 %all-to-all-start.1 = ((bf16[16,64,2048]{2,1,0:T(8,128)(2,1)}), bf16[16,64,2048]{2,1,0:T(8,128)(2,1)}, u32[]{:S(2)}, u32[]{:S(2)}) async-start(bf16[16,64,2048]{2,1,0:T(8,128)(2,1)} %convolution_convert_fusion), calls=%async_computation.1 | async-start | bytes 8388608 | tf_op jit(solution)/shard_map/all_to_all | solution.py:82
  114.0 6.3 %copy-start.2 = (bf16[2,2048,384]{2,1,0:T(8,128)(2,1)S(1)}, bf16[2,2048,384]{2,1,0:T(8,128)(2,1)}, u32[]{:S(2)}) copy-start(bf16[2,2048,384]{2,1,0:T(8,128)(2,1)} %param.15) | copy-start | bytes 9437188
  145.9 5.0 %copy-start.1 = (s32[2]{0:T(128)S(1)}, s32[2]{0:T(128)}, u32[]{:S(2)}) copy-start(s32[2]{0:T(128)} %param.21) | copy-start | bytes 28
  145.9 5.1 %copy-start.4 = (bf16[2,32,128]{2,1,0:T(8,128)(2,1)S(1)}, bf16[2,32,128]{2,1,0:T(8,128)(2,1)}, u32[]{:S(2)}) copy-start(bf16[2,32,128]{2,1,0:T(8,128)(2,1)} %param.18) | copy-start | bytes 49156
  145.9 5.8 %copy-start.3 = (bf16[2,640,4,128]{3,2,1,0:T(4,128)(2,1)S(1)}, bf16[2,640,4,128]{3,2,1,0:T(4,128)(2,1)}, u32[]{:S(2)}) copy-start(bf16[2,640,4,128]{3,2,1,0:T(4,128)(2,1)} %param.20) | copy-start | bytes 3932164
  146.0 97.5 %all-to-all-start.2 = ((bf16[16,64,2048]{2,1,0:T(8,128)(2,1)}), bf16[16,64,2048]{2,1,0:T(8,128)(2,1)}, u32[]{:S(2)}, u32[]{:S(2)}) async-start(bf16[16,64,2048]{2,1,0:T(8,128)(2,1)} %bitcast.62), calls=%async_computation.2 | async-start | bytes 8388608 | tf_op jit(solution)/shard_map/all_to_all | solution.py:96
where the time goes:
time: 248 us; the launch traced here: 247 us
  waiting for transfers between devices  183 us (74%)
  matrix products  42.8 us (17%)
  starting transfers between devices  17.7 us (7%)
    all_to_all x1, waiting for transfers between devices, local(): lax.all_to_all(outgoing, ('wide', 'narrow'), split_axis=0, concat_axis=0,...  92.4 us
    all_to_all x1, waiting for transfers between devices, local(): lax.all_to_all(result.astype(jnp.bfloat16).reshape(arrived.shape), ('wide...  90.7 us
    dot_general x2, matrix products, local(): jnp.dot(hidden, w_down[j], preferred_element_type=jnp.float32)  21.1 us
    dot_general x2, matrix products, local(): gated = jnp.dot(flat, w_gate[j], preferred_element_type=jnp.float32)  10.8 us
    all_to_all x1, starting transfers between devices, local(): lax.all_to_all(weights_out, ('wide', 'narrow'), split_axis=0, concat_axis...  6.55 us
    all_to_all x1, starting transfers between devices, local(): lax.all_to_all(outgoing, ('wide', 'narrow'), split_axis=0, concat_axis=0,...  6.12 us
    all_to_all x1, starting transfers between devices, local(): lax.all_to_all(result.astype(jnp.bfloat16).reshape(arrived.shape), ('wide...  5.03 us
  transfers between devices with their start and end apart: 3, of which 2 were waited for; matrix products, arithmetic and copies ran while one was open for 3% of the time, Pallas kernels for 0%

commit v1 on v0

--- a/solution.py
+++ b/solution.py
@@ -1,9 +1,14 @@
+import functools
 import jax
 import jax.numpy as jnp
 from jax import lax
+from jax.experimental import pallas as pl
+from jax.experimental.pallas import tpu as pltpu
 from jax.sharding import PartitionSpec as P
 
 SLOT_DEV = 2
+LANES = 128
+MESH = pl.DeviceIdType.MESH
 
 
 def attend(queries, k_cache, value_cache, lengths):
@@ -24,7 +29,7 @@
     return mixed.astype(jnp.bfloat16).reshape(reqs, heads * head_dim)
 
 
-def local(
+def exchange_local(
     tokens,
     gate_wts,
     expert_ids,
@@ -107,6 +112,393 @@
     return (routed_out, attn_out)
 
 
+def ring_place(wide, count):
+    odd = wide % 2
+    return (1 - odd) * (wide // 2) + odd * (count - 1 - wide // 2)
+
+
+def ring_wide(place, count):
+    upper = place // (count // 2)
+    return (1 - upper) * (2 * place) + upper * (2 * (count - 1 - place) + 1)
+
+
+def kernel(
+    count,
+    kv_heads,
+    x_ref,
+    coef_ref,
+    gate_hbm,
+    up_hbm,
+    down_hbm,
+    q_ref,
+    k_hbm,
+    v_hbm,
+    len_ref,
+    out_ref,
+    attn_ref,
+    xa,
+    po,
+    sb,
+    rb,
+    tb,
+    w_in,
+    w_out,
+    k_buf,
+    v_buf,
+    w_sem,
+    kv_sem,
+    ag_send,
+    ag_recv,
+    sib_send,
+    sib_recv,
+    own_send,
+    own_recv,
+    part_send,
+    part_recv,
+    part0_send,
+    part0_recv,
+    rs_send,
+    rs_recv,
+):
+    rows, width = x_ref.shape
+    half = rows // 2
+    hid = gate_hbm.shape[2]
+    arrivals = count - 1
+    wide = lax.axis_index("wide")
+    core = lax.axis_index("narrow")
+    other = 1 - core
+    place = ring_place(wide, count)
+    after = ring_wide((place + 1) % count, count)
+    before = ring_wide((place + count - 1) % count, count)
+    me = wide * 2 + core
+    targets = ({"wide": after}, {"wide": before})
+    sibling = {"narrow": other}
+
+    def aligned(index, size):
+        return pl.ds(pl.multiple_of(index * size, size), size)
+
+    def remote(src, dst, send, recv, device):
+        return pltpu.make_async_remote_copy(
+            src_ref=src, dst_ref=dst, send_sem=send, recv_sem=recv, device_id=device, device_id_type=MESH
+        )
+
+    kv_copies = [
+        pltpu.make_async_copy(k_hbm, k_buf, kv_sem.at[0]),
+        pltpu.make_async_copy(v_hbm, v_buf, kv_sem.at[1]),
+    ]
+    w_copies = []
+    for j in range(SLOT_DEV):
+        w_copies += [
+            pltpu.make_async_copy(
+                gate_hbm.at[j], w_in.at[:, pl.ds(2 * j * hid, hid)], w_sem.at[3 * j]
+            ),
+            pltpu.make_async_copy(
+                up_hbm.at[j], w_in.at[:, pl.ds((2 * j + 1) * hid, hid)], w_sem.at[3 * j + 1]
+            ),
+            pltpu.make_async_copy(
+                down_hbm.at[j], w_out.at[pl.ds(j * hid, hid)], w_sem.at[3 * j + 2]
+            ),
+        ]
+    for copy in kv_copies + w_copies:
+        copy.start()
+    xa[0, aligned(core, rows), :width] = x_ref[...]
+    xa[0, aligned(core, rows), width:] = coef_ref[...]
+
+    barrier = pltpu.get_barrier_semaphore()
+    for device in (*targets, sibling):
+        pl.semaphore_signal(barrier, inc=1, device_id=device, device_id_type=MESH)
+    pl.semaphore_wait(barrier, 3)
+
+    def unit(i, way):
+        return i + 1, aligned(way * 2 + core, half)
+
+    def gather_own(i, way):
+        piece, at = unit(i, way)
+        part = i if way == 0 else 1 - i
+        return remote(
+            xa.at[0, aligned(core * 2 + part, half)],
+            xa.at[piece, at],
+            ag_send.at[way, i],
+            ag_recv.at[way, i],
+            targets[way],
+        )
+
+    def gather_on(i, way):
+        piece, at = unit(i, way)
+        return remote(
+            xa.at[piece - 2, at], xa.at[piece, at], ag_send.at[way, i], ag_recv.at[way, i], targets[way]
+        )
+
+    def landed(i, way):
+        piece, at = unit(i, way)
+        return remote(
+            xa.at[piece, at], xa.at[piece, at], ag_send.at[way, i], ag_recv.at[way, i], targets[way]
+        )
+
+    def share(i, way):
+        piece, at = unit(i, way)
+        return remote(xa.at[piece, at], xa.at[piece, at], sib_send.at[way, i], sib_recv.at[way, i], sibling)
+
+    def share_own():
+        at = aligned(core, rows)
+        return remote(xa.at[0, at], xa.at[0, at], own_send, own_recv, sibling)
+
+    def give(i, way):
+        return remote(
+            po.at[i + 1, aligned(way * 2 + other, half)],
+            sb.at[i + 1, pl.ds(way * half, half)],
+            part_send.at[way, i],
+            part_recv.at[way, i],
+            sibling,
+        )
+
+    def give_own():
+        return remote(po.at[0, aligned(other, rows)], sb.at[0], part0_send, part0_recv, sibling)
+
+    def collect(r, way):
+        return remote(tb.at[way, r], rb.at[way, r], rs_send.at[way, r], rs_recv.at[way, r], targets[1 - way])
+
+    for i in range(2):
+        for way in range(2):
+            gather_own(i, way).start()
+    share_own().start()
+
+    for copy in kv_copies:
+        copy.wait()
+    heads, head_dim = q_ref.shape[1:]
+    group = heads // kv_heads
+    shape = (heads, k_buf.shape[1])
+    col = lax.broadcasted_iota(jnp.int32, shape, 1)
+    row = lax.broadcasted_iota(jnp.int32, shape, 0)
+    kind = jnp.zeros(shape, jnp.int32)
+    for g in range(1, kv_heads):
+        kind = kind + (row >= g * group).astype(jnp.int32)
+    mine = jnp.bitwise_and(col, kv_heads - 1) == kind
+    for r in range(q_ref.shape[0]):
+        scores = lax.dot_general(
+            q_ref[r], k_buf[r], (((1,), (1,)), ((), ())), preferred_element_type=jnp.float32
+        ) * head_dim ** (-0.5)
+        valid = mine & (col < len_ref[r] * kv_heads)
+        scores = jnp.where(valid, scores, -1e30)
+        top = jnp.max(scores, axis=-1, keepdims=True)
+        expd = jnp.where(valid, jnp.exp(scores - top), 0.0)
+        probs = (expd / jnp.sum(expd, axis=-1, keepdims=True)).astype(jnp.bfloat16)
+        mixed = jnp.dot(probs, v_buf[r], preferred_element_type=jnp.float32)
+        attn_ref[r] = mixed.astype(jnp.bfloat16)
+
+    for copy in w_copies:
+        copy.wait()
+
+    def experts(t):
+        x = xa[t, :, :width]
+        shares = xa[t, :, width:].astype(jnp.float32)
+        lane = lax.broadcasted_iota(jnp.int32, shares.shape, 1)
+        hidden = []
+        for j in range(SLOT_DEV):
+            both = jnp.dot(
+                x, w_in[:, 2 * j * hid : 2 * (j + 1) * hid], preferred_element_type=jnp.float32
+            )
+            gated, upward = both[:, :hid], both[:, hid:]
+            weight = jnp.sum(
+                jnp.where(lane == me * SLOT_DEV + j, shares, 0.0), axis=1, keepdims=True
+            )
+            hidden.append((weight * (gated / (1.0 + jnp.exp(-gated)) * upward)).astype(jnp.bfloat16))
+        hidden = jnp.concatenate(hidden, axis=1)
+        po[t] = jnp.dot(hidden, w_out[...], preferred_element_type=jnp.float32).astype(jnp.bfloat16)
+
+    def step(t, _):
+        @pl.when(t < arrivals)
+        def _():
+            for way in range(2):
+                landed(t, way).wait_recv()
+
+            @pl.when(t + 2 < arrivals)
+            def _():
+                for way in range(2):
+                    gather_on(t + 2, way).start()
+
+            for way in range(2):
+                share(t, way).start()
+
+        @pl.when(t == 0)
+        def _():
+            share_own().wait_recv()
+
+        @pl.when(t > 0)
+        def _():
+            for way in range(2):
+                share(t - 1, way).wait_recv()
+
+        experts(t)
+
+        @pl.when(t == 0)
+        def _():
+            give_own().start()
+
+        @pl.when(t > 0)
+        def _():
+            for way in range(2):
+                give(t - 1, way).start()
+
+        return _
+
+    lax.fori_loop(0, count, step, None)
+
+    def back(r, first):
+        i = arrivals - 1 - r
+        for way in range(2):
+            give(i, way).wait_recv()
+            piece, at = unit(i, way)
+            total = po[piece, at].astype(jnp.float32) + sb[piece, way * half : (way + 1) * half].astype(
+                jnp.float32
+            )
+            if not first:
+                collect(r - 2, way).wait_recv()
+                total = total + rb[way, r - 2].astype(jnp.float32)
+            tb[way, r] = total.astype(jnp.bfloat16)
+            collect(r, way).start()
+
+    for r in range(2):
+        back(r, True)
+
+    def back_on(r, _):
+        back(r, False)
+        return _
+
+    lax.fori_loop(2, arrivals, back_on, None)
+
+    give_own().wait_recv()
+    for way in range(2):
+        collect(arrivals - 2, way).wait_recv()
+        collect(arrivals - 1, way).wait_recv()
+    for part in range(2):
+        total = po[0, aligned(core * 2 + part, half)].astype(jnp.float32) + sb[
+            0, part * half : (part + 1) * half
+        ].astype(jnp.float32)
+        for way in range(2):
+            i = part if way == 0 else 1 - part
+            total = total + rb[way, arrivals - 1 - i].astype(jnp.float32)
+        out_ref[part * half : (part + 1) * half] = total.astype(jnp.bfloat16)
+
+    share_own().wait_send()
+    give_own().wait_send()
+
+    def drain(i, _):
+        for way in range(2):
+            landed(i, way).wait_send()
+            share(i, way).wait_send()
+            give(i, way).wait_send()
+            collect(i, way).wait_send()
+        return _
+
+    lax.fori_loop(0, arrivals, drain, None)
+
+
+def fused(tokens, coefs, w_gate, w_up, w_down, queries, k_cache, value_cache, lengths, budget):
+    count = lax.axis_size("wide")
+    rows, width = tokens.shape
+    half = rows // 2
+    lanes = coefs.shape[1]
+    hid = w_gate.shape[2]
+    reqs, positions, kv_heads, head_dim = k_cache.shape
+    bf16, dma = jnp.bfloat16, pltpu.SemaphoreType.DMA
+    vmem, hbm = pl.BlockSpec(memory_space=pltpu.VMEM), pl.BlockSpec(memory_space=pl.ANY)
+    arrivals = count - 1
+    pairs = dma((2, arrivals))
+    routed, attn = pl.pallas_call(
+        functools.partial(kernel, count, kv_heads),
+        out_shape=(
+            jax.ShapeDtypeStruct(tokens.shape, bf16),
+            jax.ShapeDtypeStruct(queries.shape, bf16),
+        ),
+        in_specs=[vmem, vmem, hbm, hbm, hbm, vmem, hbm, hbm, pl.BlockSpec(memory_space=pltpu.SMEM)],
+        out_specs=(vmem, vmem),
+        scratch_shapes=[
+            pltpu.VMEM((count, 2 * rows, width + lanes), bf16),
+            pltpu.VMEM((count, 2 * rows, width), bf16),
+            pltpu.VMEM((count, rows, width), bf16),
+            pltpu.VMEM((2, arrivals, half, width), bf16),
+            pltpu.VMEM((2, arrivals, half, width), bf16),
+            pltpu.VMEM((width, 2 * SLOT_DEV * hid), bf16),
+            pltpu.VMEM((SLOT_DEV * hid, width), bf16),
+            pltpu.VMEM((reqs, positions * kv_heads, head_dim), bf16),
+            pltpu.VMEM((reqs, positions * kv_heads, head_dim), bf16),
+            dma((3 * SLOT_DEV,)),
+            dma((2,)),
+            pairs,
+            pairs,
+            pairs,
+            pairs,
+            dma(()),
+            dma(()),
+            pairs,
+            pairs,
+            dma(()),
+            dma(()),
+            pairs,
+            pairs,
+        ],
+        compiler_params=pltpu.CompilerParams(
+            collective_id=0, has_side_effects=True, vmem_limit_bytes=budget
+        ),
+    )(
+        tokens,
+        coefs,
+        w_gate,
+        w_up,
+        w_down,
+        queries,
+        k_cache.reshape(reqs, positions * kv_heads, head_dim),
+        value_cache.reshape(reqs, positions * kv_heads, head_dim),
+        lengths,
+    )
+    return routed, attn.reshape(reqs, -1)
+
+
+def ring_local(budget, *args):
+    tokens, gate_wts, expert_ids, replica, w_gate, w_up, w_down, queries, k_cache, value_cache, lengths = args
+    devices = lax.axis_size("wide") * lax.axis_size("narrow")
+    experts = 3 * devices // 2
+    spares = devices // 2
+    slot = jnp.where((replica == 1) & (expert_ids < spares), expert_ids + experts, expert_ids)
+    lanes = -(-devices * SLOT_DEV // LANES) * LANES
+    named = jnp.arange(lanes, dtype=jnp.int32)
+    coefs = jnp.sum(
+        jnp.where(slot[:, :, None] == named[None, None, :], gate_wts.astype(jnp.float32)[:, :, None], 0.0),
+        axis=1,
+    ).astype(jnp.bfloat16)
+    return fused(tokens, coefs, w_gate, w_up, w_down, queries, k_cache, value_cache, lengths, budget)
+
+
+def ring_bytes(count, tokens, w_gate, k_cache):
+    rows, width = tokens.shape
+    lanes = -(-count * 2 * SLOT_DEV // LANES) * LANES
+    held = count * rows * (2 * (width + lanes) + 5 * width)
+    weights = 3 * w_gate.size
+    caches = 2 * k_cache.size
+    return 2 * (held + weights + caches)
+
+
+VMEM_BUDGET = 56 * 2**20
+VMEM_HELD = 40 * 2**20
+
+
+def local(*args):
+    count, pair = lax.axis_size("wide"), lax.axis_size("narrow")
+    kv_heads = args[8].shape[2]
+    fits = ring_bytes(count, args[0], args[4], args[8]) <= VMEM_HELD
+    shaped = (
+        pair == 2
+        and count >= 4
+        and count % 2 == 0
+        and args[0].shape[0] % 32 == 0
+        and kv_heads & (kv_heads - 1) == 0
+    )
+    if fits and shaped:
+        return ring_local(VMEM_BUDGET, *args)
+    return exchange_local(*args)
+
+
 def solution(mesh):
     in_specs = (
         P(("groups", "wide", "narrow"), None),

time: 248 us -> 61.9 us (0.25)
  the two profiles are of different devices: /device:TPU:13 before, /device:TPU:0 now
where the time goes in v1:
time: 61.9 us; the launch traced here: 61.6 us
  Pallas kernels  55.6 us (90%)
  local copies, waits for them, and re-layouts  3.86 us (6%)
  other arithmetic  1.54 us (2%)
  between operations  0.64 us (1%)
    pallas_call x1, Pallas kernels, fused(): pl.pallas_call(functools.partial(kernel, count, kv_heads), out_shape=(jax...  55.6 us
    unnamed x2, local copies, waits for them, and re-layouts  3 us

profile of v1, /device:TPU:0, one launch (start us, length us, event | category | flops | bytes accessed | tf_op | source)
XLA Modules:
  0.0 61.6 jit_solution(12506799811542305392)
XLA Ops:
  0.6 0.7 %add_select_fusion = s32[64,8]{0,1:T(8,128)S(1)} fusion(s32[64,8]{0,1:T(8,128)} %param.13, s32[64,8]{0,1:T(8,128)} %param.14), kind=kLoop, calls=%fused_computation.3 | loop fusion | flops 2560 | bytes 6144 | tf_op jit(solution)/shard_map/jit(_where)/select_n | solution.py:463
  1.3 0.1 copy.15
  1.4 0.8 %copy.16 = f32[64,8]{1,0:T(8,128)S(1)} copy(bf16[64,8]{0,1:T(8,128)(2,1)} %param.12) | data formatting | bytes 3072 | tf_op jit(solution)/shard_map/convert_element_type | solution.py:467
  2.2 0.8 %select_reduce_fusion.coef_ref = bf16[64,128]{1,0:T(8,128)(2,1)} fusion(f32[64,8]{1,0:T(8,128)S(1)} %copy.16, s32[64,8]{1,0:T(8,128)S(1)} %copy.15), kind=kLoop, calls=%fused_computation | loop fusion | flops 188416 | bytes 20480 | tf_op jit(solution)/shard_map/reduce_sum | solution.py:466
  3.0 55.6 %shard_map.122 = (bf16[64,2048]{1,0:T(8,128)(2,1)}, bf16[2,32,128]{2,1,0:T(8,128)(2,1)}) custom-call(bf16[64,2048]{1,0:T(8,128)(2,1)} %x_ref.1, bf16[64,128]{1,0:T(8,128)(2,1)} %select_reduce_fusion.coef_ref, bf16[2,2048,384]{2,1,0:T(8,128)(2,1)} %gate_hbm.1, bf16[2,2048,384]{2,1,0:T(8,128)(2,1)} %up_hbm.1, bf16[2,384,2048]{2,1,0:T(8,128)(2,1)} %down_hbm.1, ...), custom_call_target="tpu_custom_call" | custom-call | tf_op jit(solution)/shard_map/pallas_call | solution.py:408
  58.6 1.3 %copy.19 = bf16[1,2,32,128]{3,1,2,0:T(2,128)(2,1)} copy(bf16[1,2,32,128]{3,2,1,0:T(8,128)(2,1)} %bitcast.9) | data formatting | bytes 32768
  60.0 1.7 %copy.21 = bf16[64,2048]{1,0:T(8,128)(2,1)} copy(bf16[64,2048]{1,0:T(8,128)(2,1)} %get-tuple-element.8) | data formatting | bytes 524288

commit v2 on v1

--- a/solution.py
+++ b/solution.py
@@ -125,8 +125,11 @@
 def kernel(
     count,
     kv_heads,
+    lanes,
     x_ref,
-    coef_ref,
+    gate_wts_ref,
+    ids_ref,
+    replica_ref,
     gate_hbm,
     up_hbm,
     down_hbm,
@@ -201,12 +204,20 @@
         ]
     for copy in kv_copies + w_copies:
         copy.start()
-    xa[0, aligned(core, rows), :width] = x_ref[...]
-    xa[0, aligned(core, rows), width:] = coef_ref[...]
-
     barrier = pltpu.get_barrier_semaphore()
     for device in (*targets, sibling):
         pl.semaphore_signal(barrier, inc=1, device_id=device, device_id_type=MESH)
+    xa[0, aligned(core, rows), :width] = x_ref[...]
+    ids = ids_ref[...]
+    moved = (replica_ref[...] == 1) & (ids < count)
+    slot = jnp.where(moved, ids + 3 * count, ids)
+    gate_values = gate_wts_ref[...].astype(jnp.float32)
+    named = lax.broadcasted_iota(jnp.int32, (lanes, rows), 0)
+    coefs = jnp.zeros((lanes, rows), jnp.float32)
+    for k in range(ids.shape[0]):
+        coefs = coefs + jnp.where(named == slot[k : k + 1], gate_values[k : k + 1], 0.0)
+    xa[0, aligned(core, rows), width:] = coefs.T.astype(jnp.bfloat16)
+
     pl.semaphore_wait(barrier, 3)
 
     def unit(i, way):
@@ -274,6 +285,7 @@
     for g in range(1, kv_heads):
         kind = kind + (row >= g * group).astype(jnp.int32)
     mine = jnp.bitwise_and(col, kv_heads - 1) == kind
+    flat = []
     for r in range(q_ref.shape[0]):
         scores = lax.dot_general(
             q_ref[r], k_buf[r], (((1,), (1,)), ((), ())), preferred_element_type=jnp.float32
@@ -284,10 +296,8 @@
         expd = jnp.where(valid, jnp.exp(scores - top), 0.0)
         probs = (expd / jnp.sum(expd, axis=-1, keepdims=True)).astype(jnp.bfloat16)
         mixed = jnp.dot(probs, v_buf[r], preferred_element_type=jnp.float32)
-        attn_ref[r] = mixed.astype(jnp.bfloat16)
-
-    for copy in w_copies:
-        copy.wait()
+        flat.append(jnp.concatenate([mixed[h : h + 1] for h in range(heads)], axis=1))
+    attn_ref[...] = jnp.concatenate(flat, axis=0).astype(jnp.bfloat16)
 
     def experts(t):
         x = xa[t, :, :width]
@@ -306,44 +316,6 @@
         hidden = jnp.concatenate(hidden, axis=1)
         po[t] = jnp.dot(hidden, w_out[...], preferred_element_type=jnp.float32).astype(jnp.bfloat16)
 
-    def step(t, _):
-        @pl.when(t < arrivals)
-        def _():
-            for way in range(2):
-                landed(t, way).wait_recv()
-
-            @pl.when(t + 2 < arrivals)
-            def _():
-                for way in range(2):
-                    gather_on(t + 2, way).start()
-
-            for way in range(2):
-                share(t, way).start()
-
-        @pl.when(t == 0)
-        def _():
-            share_own().wait_recv()
-
-        @pl.when(t > 0)
-        def _():
-            for way in range(2):
-                share(t - 1, way).wait_recv()
-
-        experts(t)
-
-        @pl.when(t == 0)
-        def _():
-            give_own().start()
-
-        @pl.when(t > 0)
-        def _():
-            for way in range(2):
-                give(t - 1, way).start()
-
-        return _
-
-    lax.fori_loop(0, count, step, None)
-
     def back(r, first):
         i = arrivals - 1 - r
         for way in range(2):
@@ -358,8 +330,50 @@
             tb[way, r] = total.astype(jnp.bfloat16)
             collect(r, way).start()
 
-    for r in range(2):
-        back(r, True)
+    def step(t, _):
+        @pl.when(t == 0)
+        def _():
+            share_own().wait_recv()
+            for copy in w_copies:
+                copy.wait()
+
+        @pl.when(t > 0)
+        def _():
+            for way in range(2):
+                share(t - 1, way).wait_recv()
+
+        experts(t)
+
+        @pl.when(t == 0)
+        def _():
+            give_own().start()
+
+        @pl.when(t > 0)
+        def _():
+            for way in range(2):
+                give(t - 1, way).start()
+
+        @pl.when(t < arrivals)
+        def _():
+            for way in range(2):
+                landed(t, way).wait_recv()
+
+            @pl.when(t + 2 < arrivals)
+            def _():
+                for way in range(2):
+                    gather_on(t + 2, way).start()
+
+            for way in range(2):
+                share(t, way).start()
+
+        @pl.when(t == arrivals - 1)
+        def _():
+            back(1, True)
+
+        return _
+
+    lax.fori_loop(0, count, step, None)
+    back(0, True)
 
     def back_on(r, _):
         back(r, False)
@@ -394,11 +408,11 @@
     lax.fori_loop(0, arrivals, drain, None)
 
 
-def fused(tokens, coefs, w_gate, w_up, w_down, queries, k_cache, value_cache, lengths, budget):
+def fused(tokens, gate_wts, expert_ids, replica, w_gate, w_up, w_down, queries, k_cache, value_cache, lengths, budget):
     count = lax.axis_size("wide")
     rows, width = tokens.shape
     half = rows // 2
-    lanes = coefs.shape[1]
+    lanes = -(-count * 2 * SLOT_DEV // LANES) * LANES
     hid = w_gate.shape[2]
     reqs, positions, kv_heads, head_dim = k_cache.shape
     bf16, dma = jnp.bfloat16, pltpu.SemaphoreType.DMA
@@ -406,12 +420,12 @@
     arrivals = count - 1
     pairs = dma((2, arrivals))
     routed, attn = pl.pallas_call(
-        functools.partial(kernel, count, kv_heads),
+        functools.partial(kernel, count, kv_heads, lanes),
         out_shape=(
             jax.ShapeDtypeStruct(tokens.shape, bf16),
-            jax.ShapeDtypeStruct(queries.shape, bf16),
+            jax.ShapeDtypeStruct((reqs, queries.shape[1] * head_dim), bf16),
         ),
-        in_specs=[vmem, vmem, hbm, hbm, hbm, vmem, hbm, hbm, pl.BlockSpec(memory_space=pltpu.SMEM)],
+        in_specs=[vmem, vmem, vmem, vmem, hbm, hbm, hbm, vmem, hbm, hbm, pl.BlockSpec(memory_space=pltpu.SMEM)],
         out_specs=(vmem, vmem),
         scratch_shapes=[
             pltpu.VMEM((count, 2 * rows, width + lanes), bf16),
@@ -443,7 +457,9 @@
         ),
     )(
         tokens,
-        coefs,
+        gate_wts.T,
+        expert_ids.T,
+        replica.T,
         w_gate,
         w_up,
         w_down,
@@ -452,22 +468,7 @@
         value_cache.reshape(reqs, positions * kv_heads, head_dim),
         lengths,
     )
-    return routed, attn.reshape(reqs, -1)
-
-
-def ring_local(budget, *args):
-    tokens, gate_wts, expert_ids, replica, w_gate, w_up, w_down, queries, k_cache, value_cache, lengths = args
-    devices = lax.axis_size("wide") * lax.axis_size("narrow")
-    experts = 3 * devices // 2
-    spares = devices // 2
-    slot = jnp.where((replica == 1) & (expert_ids < spares), expert_ids + experts, expert_ids)
-    lanes = -(-devices * SLOT_DEV // LANES) * LANES
-    named = jnp.arange(lanes, dtype=jnp.int32)
-    coefs = jnp.sum(
-        jnp.where(slot[:, :, None] == named[None, None, :], gate_wts.astype(jnp.float32)[:, :, None], 0.0),
-        axis=1,
-    ).astype(jnp.bfloat16)
-    return fused(tokens, coefs, w_gate, w_up, w_down, queries, k_cache, value_cache, lengths, budget)
+    return routed, attn
 
 
 def ring_bytes(count, tokens, w_gate, k_cache):
@@ -495,7 +496,7 @@
         and kv_heads & (kv_heads - 1) == 0
     )
     if fits and shaped:
-        return ring_local(VMEM_BUDGET, *args)
+        return fused(*args, VMEM_BUDGET)
     return exchange_local(*args)
 
 

time: 61.9 us -> 60.2 us (0.973)
  other arithmetic: 1.54 us -> 0 us
  local copies, waits for them, and re-layouts: 3.86 us -> 3 us
  Pallas kernels: 55.6 us -> 56.3 us
    reduce_sum x1 -> x0, other arithmetic: 0.83 us -> none  [ring_local(): jnp.sum(jnp.where(slot[:, :, None] == named[None, None, :], gate_wts.asty...]
    convert_element_type x1 -> x0, local copies, waits for them, and re-layouts: 0.77 us -> none  [ring_local(): gate_wts.astype(jnp.float32)[:, :, None]]
    select_n x1 -> x0, other arithmetic: 0.71 us -> none  [ring_local(): jnp.where((replica == 1) & (expert_ids < spares), expert_ids + experts, e...]
    pallas_call x1, Pallas kernels: 55.6 us -> 56.3 us  [fused(): pl.pallas_call(functools.partial(kernel, count, kv_heads, lanes), out_sha...]
where the time goes in v2:
time: 60.2 us; the launch traced here: 59.9 us
  Pallas kernels  56.3 us (94%)
  local copies, waits for them, and re-layouts  3 us (5%)
  between operations  0.64 us (1%)
    pallas_call x1, Pallas kernels, fused(): pl.pallas_call(functools.partial(kernel, count, kv_heads, lanes), out_sha...  56.3 us
    unnamed x2, local copies, waits for them, and re-layouts  3 us

profile of v2, /device:TPU:0, one launch (start us, length us, event | category | flops | bytes accessed | tf_op | source)
XLA Modules:
  0.0 59.9 jit_solution(6721572469387138208)
XLA Ops:
  0.6 56.3 %shard_map.122 = (bf16[64,2048]{1,0:T(8,128)(2,1)}, bf16[2,4096]{1,0:T(2,128)(2,1)}) custom-call(bf16[64,2048]{1,0:T(8,128)(2,1)} %x_ref.1, bf16[8,64]{1,0:T(8,128)(2,1)} %bitcast.9, s32[8,64]{1,0:T(8,128)} %bitcast.7, s32[8,64]{1,0:T(8,128)} %bitcast.8, bf16[2,2048,384]{2,1,0:T(8,128)(2,1)} %gate_hbm.1, bf16[2,2048,384]{2,1,0:T(8,128)(2,1)} %up_hbm.1, ...), custom_call_target="tpu_custom_call" | custom-call | tf_op jit(solution)/shard_map/pallas_call | solution.py:422
  56.9 1.7 %copy.15 = bf16[64,2048]{1,0:T(8,128)(2,1)} copy(bf16[64,2048]{1,0:T(8,128)(2,1)} %get-tuple-element.4) | data formatting | bytes 524288
  58.6 1.3 %copy.16 = bf16[2,4096]{1,0:T(2,128)(2,1)} copy(bf16[2,4096]{1,0:T(2,128)(2,1)} %get-tuple-element.5) | data formatting | bytes 32768
